TPU v7x, 32 devices: a whole 2x2x4 slice. The times are simulated.
32 devices in a mesh: grp: 2 (over y), res: 8 (over z, x), ta: 2 (over core).
Axes of the slice: x: 2, y: 2, z: 4, core: 2. Of those that a mesh axis runs over, the one named last changes fastest.
Arguments:
- log_order: int32 [8, 512], P('res'), may hold values from 1 to 4096, as said below
- t_start: int32 [2], P('grp'), parts along dimension 0, may hold values from 160 to 319
- term_counts: int32 [1024], P(('grp', 'ta')), parts along dimension 0, may hold values from 4 to 32, as said below
Outputs:
- refined: float32 [2, 8, 512, 2048], P(None, None, 'res', ('grp', 'ta')), parts along dimension 3
There are 2 independent parts, one for each index of `grp`. A program takes and returns all parts, laid end to end along the dimension named above; an argument that names none is the same for every part. Nothing has to cross between parts.
Inputs may be any that keep to these rules, and one draw needn't show every extreme that they name: `log_order`: every residue 1 to 4096 appears once. `term_counts`: at least an eighth of t_m plus two, except at the first point.
All inputs are finite; a program needn't handle non-finite values.
Results may differ from a plain program's by a relative error of at most 0.00023.
Values sent between devices are 32-bit elements; how exact they have to be, the bound alone decides.
A program may use at most 64 MiB of HBM per device.

v0:
```python
import math
import jax
import jax.numpy as jnp
from jax import lax
from jax.sharding import PartitionSpec as P

TAPS = 8
MAXN = 32
time_step = 0.0625


def padded_2(block, sides, width):
    for axis, dim in sides:
        count = lax.axis_size(axis)
        forward = [(i, i + 1) for i in range(count - 1)]
        backward = [(target, source) for source, target in forward]
        low = lax.ppermute(
            lax.slice_in_dim(block, block.shape[dim] - width, None, axis=dim), axis, forward
        )
        high = lax.ppermute(lax.slice_in_dim(block, 0, width, axis=dim), axis, backward)
        block = jnp.concatenate([low, block, high], axis=dim)
    return block


def inverse_power(base_value, t_values):
    modulus = lax.rsqrt(base_value)
    phase_now = t_values * jnp.log(base_value)
    return (modulus * jnp.cos(phase_now), -modulus * jnp.sin(phase_now))


def hurwitz_values(x_values, t_values, count_row, most_terms):
    shape_out = (x_values.shape[0], t_values.shape[1])

    def add_term(term_index, running):
        sum_re, sum_im = running
        base_value = term_index.astype(x_values.dtype) + x_values
        piece_re, piece_im = inverse_power(base_value, t_values)
        active = term_index < count_row
        return (
            sum_re + jnp.where(active, piece_re, 0.0),
            sum_im + jnp.where(active, piece_im, 0.0),
        )

    zeros_init = jnp.zeros(shape_out, x_values.dtype)
    sum_re, sum_im = lax.fori_loop(0, most_terms, add_term, (zeros_init, zeros_init))
    tail_base = count_row.astype(x_values.dtype) + x_values
    power_re, power_im = inverse_power(tail_base, t_values)
    denominator = 0.25 + t_values * t_values
    lifted_re = tail_base * power_re
    lifted_im = tail_base * power_im
    total_re = sum_re + (-0.5 * lifted_re + t_values * lifted_im) / denominator + 0.5 * power_re
    total_im = sum_im + (-t_values * lifted_re - 0.5 * lifted_im) / denominator + 0.5 * power_im
    total_re = total_re + (0.5 * power_re - t_values * power_im) / (12.0 * tail_base)
    total_im = total_im + (0.5 * power_im + t_values * power_re) / (12.0 * tail_base)
    cubic_re = 1.875 - 4.5 * t_values * t_values
    cubic_im = 5.75 * t_values - t_values * t_values * t_values
    cube_base = 720.0 * tail_base * tail_base * tail_base
    total_re = total_re - (cubic_re * power_re - cubic_im * power_im) / cube_base
    total_im = total_im - (cubic_re * power_im + cubic_im * power_re) / cube_base
    return (total_re, total_im)


def sinc_value(offset):
    return math.sin(math.pi * offset) / (math.pi * offset)


def refine(padded, half_width, length):
    coarse = padded[..., half_width : half_width + length]
    middle = jnp.zeros_like(coarse)
    for offset in range(1 - half_width, half_width + 1):
        weight = sinc_value(offset - 0.5) * sinc_value((offset - 0.5) / half_width)
        middle = middle + weight * padded[..., half_width + offset : half_width + offset + length]
    stacked = jnp.stack([coarse, middle], axis=-1)
    return stacked.reshape(stacked.shape[:-2] + (2 * length,))


def matmul_high(left, right):
    return jnp.dot(left, right, precision=lax.Precision.HIGHEST, preferred_element_type=jnp.float32)


def per_device(log_order, t_start, term_counts):
    rows_here = log_order.shape[1]
    slabs = lax.axis_size("res")
    slab_index = lax.axis_index("res")
    length_here = term_counts.shape[0]
    ta_index = lax.axis_index("ta")
    modulus_int = slabs * rows_here + 1
    x_values = log_order.reshape(rows_here, 1).astype(jnp.float32) / jnp.float32(modulus_int)
    row_ids = jnp.arange(rows_here, dtype=jnp.int32)
    first_phase = (row_ids[:, None] * row_ids[None, :] % rows_here).astype(jnp.float32) * (
        2.0 * math.pi / rows_here
    )
    first_cos = jnp.cos(first_phase)
    first_sin = jnp.sin(first_phase)
    twist_phase = (row_ids * slab_index).astype(jnp.float32)[:, None] * (
        2.0 * math.pi / (slabs * rows_here)
    )
    twist_cos = jnp.cos(twist_phase)
    twist_sin = jnp.sin(twist_phase)
    slab_ids = jnp.arange(slabs, dtype=jnp.int32)
    second_phase = (slab_ids[:, None] * slab_ids[None, :] % slabs).astype(jnp.float32) * (
        2.0 * math.pi / slabs
    )
    second_cos = jnp.cos(second_phase)
    second_sin = jnp.sin(second_phase)
    positions = ta_index * length_here + jnp.arange(length_here, dtype=jnp.int32)
    count_row = term_counts[None, :]
    t_values = ((t_start[0] + positions).astype(jnp.float32) * time_step)[None, :]
    zeta_re, zeta_im = hurwitz_values(x_values, t_values, count_row, MAXN)
    mixed_re = matmul_high(first_cos, zeta_re) - matmul_high(first_sin, zeta_im)
    mixed_im = matmul_high(first_sin, zeta_re) + matmul_high(first_cos, zeta_im)
    turned_re = twist_cos * mixed_re - twist_sin * mixed_im
    turned_im = twist_sin * mixed_re + twist_cos * mixed_im
    sectioned = jnp.stack([turned_re, turned_im])[:, None]
    block_in = lax.all_to_all(sectioned, "res", split_axis=2, concat_axis=1, tiled=True)
    part_re = block_in[0]
    part_im = block_in[1]

    def mix(table, values):
        return jnp.einsum(
            "wp,psn->wsn",
            table,
            values,
            precision=lax.Precision.HIGHEST,
            preferred_element_type=jnp.float32,
        )

    out_re = mix(second_cos, part_re) - mix(second_sin, part_im)
    out_im = mix(second_sin, part_re) + mix(second_cos, part_im)
    spectrum = jnp.stack([out_re, out_im])
    factor_re, factor_im = inverse_power(jnp.float32(modulus_int), t_values)
    lval_re = spectrum[0] * factor_re - spectrum[1] * factor_im
    lval_im = spectrum[0] * factor_im + spectrum[1] * factor_re
    lvals = jnp.stack([lval_re, lval_im])
    padded = padded_2(lvals, (("ta", 3),), TAPS)
    return refine(padded, TAPS, length_here)


def solution(mesh):
    placed = (P("res", None), P("grp"), P(("grp", "ta")))
    return jax.shard_map(
        per_device,
        mesh=mesh,
        in_specs=placed,
        out_specs=P(None, None, "res", ("grp", "ta")),
        check_vma=False,
    )
```

profile of v0, /device:TPU:0, one launch (start us, length us, event | category | flops | bytes accessed | tf_op | source)
XLA Modules:
  0.0 207.3 jit_solution(16231159181828599554)
XLA Ops:
  2.1 121.0 %while.16 = (s32[]{:T(128)}, f32[512,256]{1,0:T(8,128)S(1)}, f32[512,256]{1,0:T(8,128)S(1)}, s32[1,256]{1,0:T(1,128)}, f32[512,1]{0,1:T(1,128)S(1)}, /*index=5*/s32[]{:T(128)}, s32[]{:T(128)}, s32[]{:T(128)}, s32[]{:T(128)}) while((s32[]{:T(128)}, f32[512,256]{1,0:T(8,128)S(1)}, f32[512,256]{1,0:T(8,128)S(1)}, s32[1,256]{1,0:T(1,128)}, ...), condition=%wide.region_1.2_spmd.clone, body=%wide.region_0.1_spmd.clone.sunk | while | flops 1181956 | bytes 2117255 | solution.py:45
  3.4 2.4 %fusion.139 = (f32[512,256]{1,0:T(8,128)S(1)}, f32[512,256]{1,0:T(8,128)S(1)}) fusion(f32[512,256]{1,0:T(8,128)S(1)} %get-tuple-element.249, f32[512]{0:T(512)S(1)} %neg.53, f32[512]{0:T(512)S(1)} %bitcast.58, f32[256]{0:T(256)S(1)} %bitcast.59, pred[]{:T(512)S(6)} %compare.5, pred[256]{0:T(512)(128)(4,1)S(1)} %compare_reduce_fusion.2, ...), kind=kLoop, calls=%fused_computation.8.clone.1 | loop fusion | flops 1179648 | bytes 2104577 | tf_op jit(solution)/shard_map/while/body/eval_jaxpr/add | solution.py:41
  7.2 2.4 %fusion.139 = (f32[512,256]{1,0:T(8,128)S(1)}, f32[512,256]{1,0:T(8,128)S(1)}) fusion(f32[512,256]{1,0:T(8,128)S(1)} %get-tuple-element.249, f32[512]{0:T(512)S(1)} %neg.53, f32[512]{0:T(512)S(1)} %bitcast.58, f32[256]{0:T(256)S(1)} %bitcast.59, pred[]{:T(512)S(6)} %compare.5, pred[256]{0:T(512)(128)(4,1)S(1)} %compare_reduce_fusion.2, ...), kind=kLoop, calls=%fused_computation.8.clone.1 | loop fusion | flops 1179648 | bytes 2104577 | tf_op jit(solution)/shard_map/while/body/eval_jaxpr/add | solution.py:41
  11.0 2.4 %fusion.139 = (f32[512,256]{1,0:T(8,128)S(1)}, f32[512,256]{1,0:T(8,128)S(1)}) fusion(f32[512,256]{1,0:T(8,128)S(1)} %get-tuple-element.249, f32[512]{0:T(512)S(1)} %neg.53, f32[512]{0:T(512)S(1)} %bitcast.58, f32[256]{0:T(256)S(1)} %bitcast.59, pred[]{:T(512)S(6)} %compare.5, pred[256]{0:T(512)(128)(4,1)S(1)} %compare_reduce_fusion.2, ...), kind=kLoop, calls=%fused_computation.8.clone.1 | loop fusion | flops 1179648 | bytes 2104577 | tf_op jit(solution)/shard_map/while/body/eval_jaxpr/add | solution.py:41
  14.8 2.4 %fusion.139 = (f32[512,256]{1,0:T(8,128)S(1)}, f32[512,256]{1,0:T(8,128)S(1)}) fusion(f32[512,256]{1,0:T(8,128)S(1)} %get-tuple-element.249, f32[512]{0:T(512)S(1)} %neg.53, f32[512]{0:T(512)S(1)} %bitcast.58, f32[256]{0:T(256)S(1)} %bitcast.59, pred[]{:T(512)S(6)} %compare.5, pred[256]{0:T(512)(128)(4,1)S(1)} %compare_reduce_fusion.2, ...), kind=kLoop, calls=%fused_computation.8.clone.1 | loop fusion | flops 1179648 | bytes 2104577 | tf_op jit(solution)/shard_map/while/body/eval_jaxpr/add | solution.py:41
  18.6 2.4 %fusion.139 = (f32[512,256]{1,0:T(8,128)S(1)}, f32[512,256]{1,0:T(8,128)S(1)}) fusion(f32[512,256]{1,0:T(8,128)S(1)} %get-tuple-element.249, f32[512]{0:T(512)S(1)} %neg.53, f32[512]{0:T(512)S(1)} %bitcast.58, f32[256]{0:T(256)S(1)} %bitcast.59, pred[]{:T(512)S(6)} %compare.5, pred[256]{0:T(512)(128)(4,1)S(1)} %compare_reduce_fusion.2, ...), kind=kLoop, calls=%fused_computation.8.clone.1 | loop fusion | flops 1179648 | bytes 2104577 | tf_op jit(solution)/shard_map/while/body/eval_jaxpr/add | solution.py:41
  22.4 2.4 %fusion.139 = (f32[512,256]{1,0:T(8,128)S(1)}, f32[512,256]{1,0:T(8,128)S(1)}) fusion(f32[512,256]{1,0:T(8,128)S(1)} %get-tuple-element.249, f32[512]{0:T(512)S(1)} %neg.53, f32[512]{0:T(512)S(1)} %bitcast.58, f32[256]{0:T(256)S(1)} %bitcast.59, pred[]{:T(512)S(6)} %compare.5, pred[256]{0:T(512)(128)(4,1)S(1)} %compare_reduce_fusion.2, ...), kind=kLoop, calls=%fused_computation.8.clone.1 | loop fusion | flops 1179648 | bytes 2104577 | tf_op jit(solution)/shard_map/while/body/eval_jaxpr/add | solution.py:41
  26.1 2.4 %fusion.139 = (f32[512,256]{1,0:T(8,128)S(1)}, f32[512,256]{1,0:T(8,128)S(1)}) fusion(f32[512,256]{1,0:T(8,128)S(1)} %get-tuple-element.249, f32[512]{0:T(512)S(1)} %neg.53, f32[512]{0:T(512)S(1)} %bitcast.58, f32[256]{0:T(256)S(1)} %bitcast.59, pred[]{:T(512)S(6)} %compare.5, pred[256]{0:T(512)(128)(4,1)S(1)} %compare_reduce_fusion.2, ...), kind=kLoop, calls=%fused_computation.8.clone.1 | loop fusion | flops 1179648 | bytes 2104577 | tf_op jit(solution)/shard_map/while/body/eval_jaxpr/add | solution.py:41
  29.9 2.4 %fusion.139 = (f32[512,256]{1,0:T(8,128)S(1)}, f32[512,256]{1,0:T(8,128)S(1)}) fusion(f32[512,256]{1,0:T(8,128)S(1)} %get-tuple-element.249, f32[512]{0:T(512)S(1)} %neg.53, f32[512]{0:T(512)S(1)} %bitcast.58, f32[256]{0:T(256)S(1)} %bitcast.59, pred[]{:T(512)S(6)} %compare.5, pred[256]{0:T(512)(128)(4,1)S(1)} %compare_reduce_fusion.2, ...), kind=kLoop, calls=%fused_computation.8.clone.1 | loop fusion | flops 1179648 | bytes 2104577 | tf_op jit(solution)/shard_map/while/body/eval_jaxpr/add | solution.py:41
  33.7 2.4 %fusion.139 = (f32[512,256]{1,0:T(8,128)S(1)}, f32[512,256]{1,0:T(8,128)S(1)}) fusion(f32[512,256]{1,0:T(8,128)S(1)} %get-tuple-element.249, f32[512]{0:T(512)S(1)} %neg.53, f32[512]{0:T(512)S(1)} %bitcast.58, f32[256]{0:T(256)S(1)} %bitcast.59, pred[]{:T(512)S(6)} %compare.5, pred[256]{0:T(512)(128)(4,1)S(1)} %compare_reduce_fusion.2, ...), kind=kLoop, calls=%fused_computation.8.clone.1 | loop fusion | flops 1179648 | bytes 2104577 | tf_op jit(solution)/shard_map/while/body/eval_jaxpr/add | solution.py:41
  37.5 2.4 %fusion.139 = (f32[512,256]{1,0:T(8,128)S(1)}, f32[512,256]{1,0:T(8,128)S(1)}) fusion(f32[512,256]{1,0:T(8,128)S(1)} %get-tuple-element.249, f32[512]{0:T(512)S(1)} %neg.53, f32[512]{0:T(512)S(1)} %bitcast.58, f32[256]{0:T(256)S(1)} %bitcast.59, pred[]{:T(512)S(6)} %compare.5, pred[256]{0:T(512)(128)(4,1)S(1)} %compare_reduce_fusion.2, ...), kind=kLoop, calls=%fused_computation.8.clone.1 | loop fusion | flops 1179648 | bytes 2104577 | tf_op jit(solution)/shard_map/while/body/eval_jaxpr/add | solution.py:41
  41.3 2.4 %fusion.139 = (f32[512,256]{1,0:T(8,128)S(1)}, f32[512,256]{1,0:T(8,128)S(1)}) fusion(f32[512,256]{1,0:T(8,128)S(1)} %get-tuple-element.249, f32[512]{0:T(512)S(1)} %neg.53, f32[512]{0:T(512)S(1)} %bitcast.58, f32[256]{0:T(256)S(1)} %bitcast.59, pred[]{:T(512)S(6)} %compare.5, pred[256]{0:T(512)(128)(4,1)S(1)} %compare_reduce_fusion.2, ...), kind=kLoop, calls=%fused_computation.8.clone.1 | loop fusion | flops 1179648 | bytes 2104577 | tf_op jit(solution)/shard_map/while/body/eval_jaxpr/add | solution.py:41
  45.1 2.4 %fusion.139 = (f32[512,256]{1,0:T(8,128)S(1)}, f32[512,256]{1,0:T(8,128)S(1)}) fusion(f32[512,256]{1,0:T(8,128)S(1)} %get-tuple-element.249, f32[512]{0:T(512)S(1)} %neg.53, f32[512]{0:T(512)S(1)} %bitcast.58, f32[256]{0:T(256)S(1)} %bitcast.59, pred[]{:T(512)S(6)} %compare.5, pred[256]{0:T(512)(128)(4,1)S(1)} %compare_reduce_fusion.2, ...), kind=kLoop, calls=%fused_computation.8.clone.1 | loop fusion | flops 1179648 | bytes 2104577 | tf_op jit(solution)/shard_map/while/body/eval_jaxpr/add | solution.py:41
  48.8 2.4 %fusion.139 = (f32[512,256]{1,0:T(8,128)S(1)}, f32[512,256]{1,0:T(8,128)S(1)}) fusion(f32[512,256]{1,0:T(8,128)S(1)} %get-tuple-element.249, f32[512]{0:T(512)S(1)} %neg.53, f32[512]{0:T(512)S(1)} %bitcast.58, f32[256]{0:T(256)S(1)} %bitcast.59, pred[]{:T(512)S(6)} %compare.5, pred[256]{0:T(512)(128)(4,1)S(1)} %compare_reduce_fusion.2, ...), kind=kLoop, calls=%fused_computation.8.clone.1 | loop fusion | flops 1179648 | bytes 2104577 | tf_op jit(solution)/shard_map/while/body/eval_jaxpr/add | solution.py:41
  52.6 2.4 %fusion.139 = (f32[512,256]{1,0:T(8,128)S(1)}, f32[512,256]{1,0:T(8,128)S(1)}) fusion(f32[512,256]{1,0:T(8,128)S(1)} %get-tuple-element.249, f32[512]{0:T(512)S(1)} %neg.53, f32[512]{0:T(512)S(1)} %bitcast.58, f32[256]{0:T(256)S(1)} %bitcast.59, pred[]{:T(512)S(6)} %compare.5, pred[256]{0:T(512)(128)(4,1)S(1)} %compare_reduce_fusion.2, ...), kind=kLoop, calls=%fused_computation.8.clone.1 | loop fusion | flops 1179648 | bytes 2104577 | tf_op jit(solution)/shard_map/while/body/eval_jaxpr/add | solution.py:41
  56.4 2.4 %fusion.139 = (f32[512,256]{1,0:T(8,128)S(1)}, f32[512,256]{1,0:T(8,128)S(1)}) fusion(f32[512,256]{1,0:T(8,128)S(1)} %get-tuple-element.249, f32[512]{0:T(512)S(1)} %neg.53, f32[512]{0:T(512)S(1)} %bitcast.58, f32[256]{0:T(256)S(1)} %bitcast.59, pred[]{:T(512)S(6)} %compare.5, pred[256]{0:T(512)(128)(4,1)S(1)} %compare_reduce_fusion.2, ...), kind=kLoop, calls=%fused_computation.8.clone.1 | loop fusion | flops 1179648 | bytes 2104577 | tf_op jit(solution)/shard_map/while/body/eval_jaxpr/add | solution.py:41
  60.2 2.4 %fusion.139 = (f32[512,256]{1,0:T(8,128)S(1)}, f32[512,256]{1,0:T(8,128)S(1)}) fusion(f32[512,256]{1,0:T(8,128)S(1)} %get-tuple-element.249, f32[512]{0:T(512)S(1)} %neg.53, f32[512]{0:T(512)S(1)} %bitcast.58, f32[256]{0:T(256)S(1)} %bitcast.59, pred[]{:T(512)S(6)} %compare.5, pred[256]{0:T(512)(128)(4,1)S(1)} %compare_reduce_fusion.2, ...), kind=kLoop, calls=%fused_computation.8.clone.1 | loop fusion | flops 1179648 | bytes 2104577 | tf_op jit(solution)/shard_map/while/body/eval_jaxpr/add | solution.py:41
  64.0 2.4 %fusion.139 = (f32[512,256]{1,0:T(8,128)S(1)}, f32[512,256]{1,0:T(8,128)S(1)}) fusion(f32[512,256]{1,0:T(8,128)S(1)} %get-tuple-element.249, f32[512]{0:T(512)S(1)} %neg.53, f32[512]{0:T(512)S(1)} %bitcast.58, f32[256]{0:T(256)S(1)} %bitcast.59, pred[]{:T(512)S(6)} %compare.5, pred[256]{0:T(512)(128)(4,1)S(1)} %compare_reduce_fusion.2, ...), kind=kLoop, calls=%fused_computation.8.clone.1 | loop fusion | flops 1179648 | bytes 2104577 | tf_op jit(solution)/shard_map/while/body/eval_jaxpr/add | solution.py:41
  67.8 2.4 %fusion.139 = (f32[512,256]{1,0:T(8,128)S(1)}, f32[512,256]{1,0:T(8,128)S(1)}) fusion(f32[512,256]{1,0:T(8,128)S(1)} %get-tuple-element.249, f32[512]{0:T(512)S(1)} %neg.53, f32[512]{0:T(512)S(1)} %bitcast.58, f32[256]{0:T(256)S(1)} %bitcast.59, pred[]{:T(512)S(6)} %compare.5, pred[256]{0:T(512)(128)(4,1)S(1)} %compare_reduce_fusion.2, ...), kind=kLoop, calls=%fused_computation.8.clone.1 | loop fusion | flops 1179648 | bytes 2104577 | tf_op jit(solution)/shard_map/while/body/eval_jaxpr/add | solution.py:41
  71.5 2.4 %fusion.139 = (f32[512,256]{1,0:T(8,128)S(1)}, f32[512,256]{1,0:T(8,128)S(1)}) fusion(f32[512,256]{1,0:T(8,128)S(1)} %get-tuple-element.249, f32[512]{0:T(512)S(1)} %neg.53, f32[512]{0:T(512)S(1)} %bitcast.58, f32[256]{0:T(256)S(1)} %bitcast.59, pred[]{:T(512)S(6)} %compare.5, pred[256]{0:T(512)(128)(4,1)S(1)} %compare_reduce_fusion.2, ...), kind=kLoop, calls=%fused_computation.8.clone.1 | loop fusion | flops 1179648 | bytes 2104577 | tf_op jit(solution)/shard_map/while/body/eval_jaxpr/add | solution.py:41
  75.3 2.4 %fusion.139 = (f32[512,256]{1,0:T(8,128)S(1)}, f32[512,256]{1,0:T(8,128)S(1)}) fusion(f32[512,256]{1,0:T(8,128)S(1)} %get-tuple-element.249, f32[512]{0:T(512)S(1)} %neg.53, f32[512]{0:T(512)S(1)} %bitcast.58, f32[256]{0:T(256)S(1)} %bitcast.59, pred[]{:T(512)S(6)} %compare.5, pred[256]{0:T(512)(128)(4,1)S(1)} %compare_reduce_fusion.2, ...), kind=kLoop, calls=%fused_computation.8.clone.1 | loop fusion | flops 1179648 | bytes 2104577 | tf_op jit(solution)/shard_map/while/body/eval_jaxpr/add | solution.py:41
  79.1 2.4 %fusion.139 = (f32[512,256]{1,0:T(8,128)S(1)}, f32[512,256]{1,0:T(8,128)S(1)}) fusion(f32[512,256]{1,0:T(8,128)S(1)} %get-tuple-element.249, f32[512]{0:T(512)S(1)} %neg.53, f32[512]{0:T(512)S(1)} %bitcast.58, f32[256]{0:T(256)S(1)} %bitcast.59, pred[]{:T(512)S(6)} %compare.5, pred[256]{0:T(512)(128)(4,1)S(1)} %compare_reduce_fusion.2, ...), kind=kLoop, calls=%fused_computation.8.clone.1 | loop fusion | flops 1179648 | bytes 2104577 | tf_op jit(solution)/shard_map/while/body/eval_jaxpr/add | solution.py:41
  82.9 2.4 %fusion.139 = (f32[512,256]{1,0:T(8,128)S(1)}, f32[512,256]{1,0:T(8,128)S(1)}) fusion(f32[512,256]{1,0:T(8,128)S(1)} %get-tuple-element.249, f32[512]{0:T(512)S(1)} %neg.53, f32[512]{0:T(512)S(1)} %bitcast.58, f32[256]{0:T(256)S(1)} %bitcast.59, pred[]{:T(512)S(6)} %compare.5, pred[256]{0:T(512)(128)(4,1)S(1)} %compare_reduce_fusion.2, ...), kind=kLoop, calls=%fused_computation.8.clone.1 | loop fusion | flops 1179648 | bytes 2104577 | tf_op jit(solution)/shard_map/while/body/eval_jaxpr/add | solution.py:41
  86.7 2.4 %fusion.139 = (f32[512,256]{1,0:T(8,128)S(1)}, f32[512,256]{1,0:T(8,128)S(1)}) fusion(f32[512,256]{1,0:T(8,128)S(1)} %get-tuple-element.249, f32[512]{0:T(512)S(1)} %neg.53, f32[512]{0:T(512)S(1)} %bitcast.58, f32[256]{0:T(256)S(1)} %bitcast.59, pred[]{:T(512)S(6)} %compare.5, pred[256]{0:T(512)(128)(4,1)S(1)} %compare_reduce_fusion.2, ...), kind=kLoop, calls=%fused_computation.8.clone.1 | loop fusion | flops 1179648 | bytes 2104577 | tf_op jit(solution)/shard_map/while/body/eval_jaxpr/add | solution.py:41
  90.4 2.4 %fusion.139 = (f32[512,256]{1,0:T(8,128)S(1)}, f32[512,256]{1,0:T(8,128)S(1)}) fusion(f32[512,256]{1,0:T(8,128)S(1)} %get-tuple-element.249, f32[512]{0:T(512)S(1)} %neg.53, f32[512]{0:T(512)S(1)} %bitcast.58, f32[256]{0:T(256)S(1)} %bitcast.59, pred[]{:T(512)S(6)} %compare.5, pred[256]{0:T(512)(128)(4,1)S(1)} %compare_reduce_fusion.2, ...), kind=kLoop, calls=%fused_computation.8.clone.1 | loop fusion | flops 1179648 | bytes 2104577 | tf_op jit(solution)/shard_map/while/body/eval_jaxpr/add | solution.py:41
  94.2 2.4 %fusion.139 = (f32[512,256]{1,0:T(8,128)S(1)}, f32[512,256]{1,0:T(8,128)S(1)}) fusion(f32[512,256]{1,0:T(8,128)S(1)} %get-tuple-element.249, f32[512]{0:T(512)S(1)} %neg.53, f32[512]{0:T(512)S(1)} %bitcast.58, f32[256]{0:T(256)S(1)} %bitcast.59, pred[]{:T(512)S(6)} %compare.5, pred[256]{0:T(512)(128)(4,1)S(1)} %compare_reduce_fusion.2, ...), kind=kLoop, calls=%fused_computation.8.clone.1 | loop fusion | flops 1179648 | bytes 2104577 | tf_op jit(solution)/shard_map/while/body/eval_jaxpr/add | solution.py:41
  98.0 2.4 %fusion.139 = (f32[512,256]{1,0:T(8,128)S(1)}, f32[512,256]{1,0:T(8,128)S(1)}) fusion(f32[512,256]{1,0:T(8,128)S(1)} %get-tuple-element.249, f32[512]{0:T(512)S(1)} %neg.53, f32[512]{0:T(512)S(1)} %bitcast.58, f32[256]{0:T(256)S(1)} %bitcast.59, pred[]{:T(512)S(6)} %compare.5, pred[256]{0:T(512)(128)(4,1)S(1)} %compare_reduce_fusion.2, ...), kind=kLoop, calls=%fused_computation.8.clone.1 | loop fusion | flops 1179648 | bytes 2104577 | tf_op jit(solution)/shard_map/while/body/eval_jaxpr/add | solution.py:41
  101.8 2.4 %fusion.139 = (f32[512,256]{1,0:T(8,128)S(1)}, f32[512,256]{1,0:T(8,128)S(1)}) fusion(f32[512,256]{1,0:T(8,128)S(1)} %get-tuple-element.249, f32[512]{0:T(512)S(1)} %neg.53, f32[512]{0:T(512)S(1)} %bitcast.58, f32[256]{0:T(256)S(1)} %bitcast.59, pred[]{:T(512)S(6)} %compare.5, pred[256]{0:T(512)(128)(4,1)S(1)} %compare_reduce_fusion.2, ...), kind=kLoop, calls=%fused_computation.8.clone.1 | loop fusion | flops 1179648 | bytes 2104577 | tf_op jit(solution)/shard_map/while/body/eval_jaxpr/add | solution.py:41
  105.6 2.4 %fusion.139 = (f32[512,256]{1,0:T(8,128)S(1)}, f32[512,256]{1,0:T(8,128)S(1)}) fusion(f32[512,256]{1,0:T(8,128)S(1)} %get-tuple-element.249, f32[512]{0:T(512)S(1)} %neg.53, f32[512]{0:T(512)S(1)} %bitcast.58, f32[256]{0:T(256)S(1)} %bitcast.59, pred[]{:T(512)S(6)} %compare.5, pred[256]{0:T(512)(128)(4,1)S(1)} %compare_reduce_fusion.2, ...), kind=kLoop, calls=%fused_computation.8.clone.1 | loop fusion | flops 1179648 | bytes 2104577 | tf_op jit(solution)/shard_map/while/body/eval_jaxpr/add | solution.py:41
  109.4 2.4 %fusion.139 = (f32[512,256]{1,0:T(8,128)S(1)}, f32[512,256]{1,0:T(8,128)S(1)}) fusion(f32[512,256]{1,0:T(8,128)S(1)} %get-tuple-element.249, f32[512]{0:T(512)S(1)} %neg.53, f32[512]{0:T(512)S(1)} %bitcast.58, f32[256]{0:T(256)S(1)} %bitcast.59, pred[]{:T(512)S(6)} %compare.5, pred[256]{0:T(512)(128)(4,1)S(1)} %compare_reduce_fusion.2, ...), kind=kLoop, calls=%fused_computation.8.clone.1 | loop fusion | flops 1179648 | bytes 2104577 | tf_op jit(solution)/shard_map/while/body/eval_jaxpr/add | solution.py:41
  113.1 2.4 %fusion.139 = (f32[512,256]{1,0:T(8,128)S(1)}, f32[512,256]{1,0:T(8,128)S(1)}) fusion(f32[512,256]{1,0:T(8,128)S(1)} %get-tuple-element.249, f32[512]{0:T(512)S(1)} %neg.53, f32[512]{0:T(512)S(1)} %bitcast.58, f32[256]{0:T(256)S(1)} %bitcast.59, pred[]{:T(512)S(6)} %compare.5, pred[256]{0:T(512)(128)(4,1)S(1)} %compare_reduce_fusion.2, ...), kind=kLoop, calls=%fused_computation.8.clone.1 | loop fusion | flops 1179648 | bytes 2104577 | tf_op jit(solution)/shard_map/while/body/eval_jaxpr/add | solution.py:41
  116.9 2.4 %fusion.139 = (f32[512,256]{1,0:T(8,128)S(1)}, f32[512,256]{1,0:T(8,128)S(1)}) fusion(f32[512,256]{1,0:T(8,128)S(1)} %get-tuple-element.249, f32[512]{0:T(512)S(1)} %neg.53, f32[512]{0:T(512)S(1)} %bitcast.58, f32[256]{0:T(256)S(1)} %bitcast.59, pred[]{:T(512)S(6)} %compare.5, pred[256]{0:T(512)(128)(4,1)S(1)} %compare_reduce_fusion.2, ...), kind=kLoop, calls=%fused_computation.8.clone.1 | loop fusion | flops 1179648 | bytes 2104577 | tf_op jit(solution)/shard_map/while/body/eval_jaxpr/add | solution.py:41
  120.7 2.4 %fusion.139 = (f32[512,256]{1,0:T(8,128)S(1)}, f32[512,256]{1,0:T(8,128)S(1)}) fusion(f32[512,256]{1,0:T(8,128)S(1)} %get-tuple-element.249, f32[512]{0:T(512)S(1)} %neg.53, f32[512]{0:T(512)S(1)} %bitcast.58, f32[256]{0:T(256)S(1)} %bitcast.59, pred[]{:T(512)S(6)} %compare.5, pred[256]{0:T(512)(128)(4,1)S(1)} %compare_reduce_fusion.2, ...), kind=kLoop, calls=%fused_computation.8.clone.1 | loop fusion | flops 1179648 | bytes 2104577 | tf_op jit(solution)/shard_map/while/body/eval_jaxpr/add | solution.py:41
  123.1 2.9 %fusion.38 = (f32[512,256]{1,0:T(8,128)S(1)}, f32[512,256]{1,0:T(8,128)S(1)}) fusion(f32[512,256]{1,0:T(8,128)S(1)} %get-tuple-element.116, f32[256]{0:T(256)S(1)} %fusion.93, f32[256]{0:T(256)S(1)} %get-tuple-element.180, f32[256]{0:T(256)S(1)} %get-tuple-element.183, f32[256]{0:T(256)S(1)} %get-tuple-element.179, f32[256]{0:T(256)S(1)} %get-tuple-element.184, ...), kind=kLoop, calls=%fused_computation.82 | loop fusion | flops 5636096 | bytes 2105344 | tf_op jit(solution)/shard_map/sub | solution.py:59
  126.0 5.6 %fusion.65 = f32[512,256]{1,0:T(8,128)S(1)} fusion(f32[512,256]{1,0:T(8,128)S(1)} %get-tuple-element.176), kind=kOutput, calls=%fused_computation.111 | convolution fusion | flops 808976384 | bytes 1048576 | tf_op jit(solution)/shard_map/dot_general | solution.py:78
  131.6 5.6 %fusion.63 = f32[512,256]{1,0:T(8,128)S(1)} fusion(f32[512,256]{1,0:T(8,128)S(1)} %get-tuple-element.176), kind=kOutput, calls=%fused_computation.110 | convolution fusion | flops 808976384 | bytes 1048576 | tf_op jit(solution)/shard_map/dot_general | solution.py:78
  137.3 5.6 %convolution_add_fusion = f32[512,256]{1,0:T(8,128)S(1)} fusion(f32[512,256]{1,0:T(8,128)S(1)} %fusion.65, f32[512,256]{1,0:T(8,128)S(1)} %get-tuple-element.175), kind=kOutput, calls=%fused_computation.32 | convolution fusion | flops 809107456 | bytes 1572864 | tf_op jit(solution)/shard_map/dot_general | solution.py:78
  142.9 7.2 %subtract_bitcast_fusion.1 = (f32[1,512,256]{2,1,0:T(8,128)S(1)}, f32[1,512,256]{2,1,0:T(8,128)S(1)}) fusion(f32[512,256]{1,0:T(8,128)S(1)} %convolution_add_fusion, f32[512]{0:T(512)S(1)} %get-tuple-element.185, f32[512]{0:T(512)S(1)} %get-tuple-element.186, f32[512,256]{1,0:T(8,128)S(1)} %fusion.63, f32[512,256]{1,0:T(8,128)S(1)} %get-tuple-element.175), kind=kOutput, calls=%fused_computation.107 | convolution fusion | flops 809893888 | bytes 2625536 | tf_op jit(solution)/shard_map/dot_general | solution.py:78
  150.2 1.8 copy.17
  152.0 7.3 %all-to-all-start = ((f32[2,1,512,256]{3,0,1,2:T(2,128)}), f32[2,1,512,256]{3,0,1,2:T(2,128)S(1)}, u32[]{:S(2)}, u32[]{:S(2)}) async-start(f32[2,1,512,256]{3,0,1,2:T(2,128)} %copy.17), calls=%async_computation | async-start | bytes 2097152 | tf_op jit(solution)/shard_map/all_to_all | solution.py:115
  159.3 25.7 %all-to-all-done = f32[2,1,512,256]{3,0,1,2:T(2,128)S(1)} async-done(((f32[2,1,512,256]{3,0,1,2:T(2,128)}), f32[2,1,512,256]{3,0,1,2:T(2,128)S(1)}, u32[]{:S(2)}, u32[]{:S(2)}) %all-to-all-start) | async-done | bytes 1048608 | tf_op jit(solution)/shard_map/all_to_all | solution.py:115
  188.4 1.0 add_bitcast_fusion
  189.6 1.3 collective-permute-start
  190.9 1.3 collective-permute-start.1
  192.4 2.3 %collective-permute-done.1 = f32[2,8,64,8]{3,1,2,0:T(8,128)S(1)} collective-permute-done((f32[2,8,64,8]{3,1,2,0:T(8,128)S(1)}, f32[2,8,64,8]{3,1,2,0:T(8,128)S(1)}, u32[]{:S(2)}, u32[]{:S(2)}) %collective-permute-start.1) | collective-permute-done | bytes 32800 | tf_op jit(solution)/shard_map/ppermute | solution.py:20
  195.2 4.2 %fusion.30 = (f32[2,8,64,256,1]{3,1,2,0,4:T(8,128)S(1)}, f32[2,8,64,256,1]{3,1,2,0,4:T(8,128)S(1)}) fusion(f32[1,8,64,256]{3,1,2,0:T(8,128)S(1)} %get-tuple-element.165, f32[1,8,64,256]{3,1,2,0:T(8,128)S(1)} %get-tuple-element.166, f32[2,8,64,264]{3,1,2,0:T(8,128)S(1)} %get-tuple-element.170, f32[2,8,64,264]{3,1,2,0:T(8,128)S(1)} %get-tuple-element.169), kind=kLoop, calls=%fused_computation.74 | loop fusion | flops 8388608 | bytes 18874368 | tf_op jit(solution)/shard_map/stack | solution.py:73
  199.6 3.9 %copy.24 = f32[2,8,64,256,2]{2,1,4,3,0:T(8,128)} copy(f32[2,8,64,256,2]{3,1,2,0,4:T(8,128)S(1)} %pad_maximum_fusion) | data formatting | bytes 4194304 | tf_op jit(solution)/shard_map/stack | solution.py:73
  203.5 3.8 %copy.25 = f32[2,8,64,512]{3,2,1,0:T(8,128)} copy(f32[2,8,64,512]{2,1,3,0:T(8,128)} %bitcast.51) | data formatting | bytes 4194304 | tf_op jit(solution)/shard_map/reshape | solution.py:74
  (148 shorter events, 49.9 us)
Async XLA Ops:
  152.0 33.0 %all-to-all-start = ((f32[2,1,512,256]{3,0,1,2:T(2,128)}), f32[2,1,512,256]{3,0,1,2:T(2,128)S(1)}, u32[]{:S(2)}, u32[]{:S(2)}) async-start(f32[2,1,512,256]{3,0,1,2:T(2,128)} %copy.17), calls=%async_computation | async-start | bytes 2097152 | tf_op jit(solution)/shard_map/all_to_all | solution.py:115
  189.6 2.8 %collective-permute-start = (f32[2,8,64,8]{3,1,2,0:T(8,128)S(1)}, f32[2,8,64,8]{3,1,2,0:T(8,128)S(1)}, u32[]{:S(2)}, u32[]{:S(2)}) collective-permute-start(f32[2,8,64,8]{3,1,2,0:T(8,128)S(1)} %get-tuple-element.171), channel_id=1, source_target_pairs={{0,1},{2,3},{4,5},{6,7},{8,9},{10,11},{12,13},{14,15},{16,17},{18,... | collective-permute-start | bytes 98312 | tf_op jit(solution)/shard_map/ppermute | solution.py:17
  190.9 3.8 %collective-permute-start.1 = (f32[2,8,64,8]{3,1,2,0:T(8,128)S(1)}, f32[2,8,64,8]{3,1,2,0:T(8,128)S(1)}, u32[]{:S(2)}, u32[]{:S(2)}) collective-permute-start(f32[2,8,64,8]{3,1,2,0:T(8,128)S(1)} %get-tuple-element.172), channel_id=1, source_target_pairs={{1,0},{3,2},{5,4},{7,6},{9,8},{11,10},{13,12},{15,14},{17,16},{19,... | collective-permute-start | bytes 98312 | tf_op jit(solution)/shard_map/ppermute | solution.py:20
where the time goes:
time: 210 us; the launch traced here: 207 us
  other arithmetic  129 us (61%)
  waiting for transfers between devices  28.2 us (13%)
  matrix products  27.5 us (13%)
  local copies, waits for them, and re-layouts  10.4 us (5%)
  starting transfers between devices  9.87 us (5%)
    add x32, other arithmetic, add_term(): sum_im + jnp.where(active, piece_im, 0.0)  75.7 us
    all_to_all x1, waiting for transfers between devices, per_device(): lax.all_to_all(sectioned, 'res', split_axis=2, concat_axis=1, tiled=True)  25.7 us
    dot_general x4, matrix products, matmul_high(): jnp.dot(left, right, precision=lax.Precision.HIGHEST, preferred_element_t...  24.1 us
    lt x32, other arithmetic, add_term(): active = term_index < count_row  22.4 us
    mul x32, other arithmetic, per_device(): (t_start[0] + positions).astype(jnp.float32) * time_step  20.9 us
    all_to_all x1, starting transfers between devices, per_device(): lax.all_to_all(sectioned, 'res', split_axis=2, concat_axis=1, tiled=True)  7.26 us
    another operation x2, other arithmetic, refine(): stacked = jnp.stack([coarse, middle], axis=-1)  4.36 us
  transfers between devices with their start and end apart: 3, of which 3 were waited for; matrix products, arithmetic and copies ran while one was open for 0% of the time, Pallas kernels for 0%

commit v1 on v0

--- a/solution.py
+++ b/solution.py
@@ -112,7 +112,9 @@
     turned_re = twist_cos * mixed_re - twist_sin * mixed_im
     turned_im = twist_sin * mixed_re + twist_cos * mixed_im
     sectioned = jnp.stack([turned_re, turned_im])[:, None]
-    block_in = lax.all_to_all(sectioned, "res", split_axis=2, concat_axis=1, tiled=True)
+    shards = jnp.split(sectioned, lax.axis_size("res"), axis=2)
+    received = lax.all_to_all(jnp.stack(shards), "res", 0, 0)
+    block_in = jnp.concatenate(received, axis=1)
     part_re = block_in[0]
     part_im = block_in[1]
 

time: 210 us -> 213 us (1.014)
  local copies, waits for them, and re-layouts: 10.4 us -> 13.1 us
    unnamed x2 -> x7, local copies, waits for them, and re-layouts: 0.07 us -> 4.65 us
where the time goes in v1:
time: 213 us; the launch traced here: 210 us
  other arithmetic  129 us (61%)
  waiting for transfers between devices  28.2 us (13%)
  matrix products  27.5 us (13%)
  local copies, waits for them, and re-layouts  13.1 us (6%)
  starting transfers between devices  9.87 us (5%)
    add x32, other arithmetic, add_term(): sum_im + jnp.where(active, piece_im, 0.0)  75.7 us
    all_to_all x1, waiting for transfers between devices, per_device(): received = lax.all_to_all(jnp.stack(shards), 'res', 0, 0)  25.7 us
    dot_general x4, matrix products, matmul_high(): jnp.dot(left, right, precision=lax.Precision.HIGHEST, preferred_element_t...  24.1 us
    lt x32, other arithmetic, add_term(): active = term_index < count_row  22.4 us
    mul x32, other arithmetic, per_device(): (t_start[0] + positions).astype(jnp.float32) * time_step  20.9 us
    all_to_all x1, starting transfers between devices, per_device(): received = lax.all_to_all(jnp.stack(shards), 'res', 0, 0)  7.26 us
    unnamed x7, local copies, waits for them, and re-layouts  4.65 us
    another operation x2, other arithmetic, refine(): stacked = jnp.stack([coarse, middle], axis=-1)  4.36 us
  transfers between devices with their start and end apart: 3, of which 3 were waited for; matrix products, arithmetic and copies ran while one was open for 0% of the time, Pallas kernels for 0%

profile of v1, /device:TPU:0, one launch (start us, length us, event | category | flops | bytes accessed | tf_op | source)
XLA Modules:
  0.0 210.0 jit_solution(12155001008396109148)
XLA Ops:
  2.1 121.0 %while.16 = (s32[]{:T(128)}, f32[512,256]{1,0:T(8,128)S(1)}, f32[512,256]{1,0:T(8,128)S(1)}, s32[1,256]{1,0:T(1,128)}, f32[512,1]{0,1:T(1,128)S(1)}, /*index=5*/s32[]{:T(128)}, s32[]{:T(128)}, s32[]{:T(128)}, s32[]{:T(128)}) while((s32[]{:T(128)}, f32[512,256]{1,0:T(8,128)S(1)}, f32[512,256]{1,0:T(8,128)S(1)}, s32[1,256]{1,0:T(1,128)}, ...), condition=%wide.region_1.2_spmd.clone, body=%wide.region_0.1_spmd.clone.sunk | while | flops 1181956 | bytes 2117255 | solution.py:45
  3.4 2.4 %fusion.146 = (f32[512,256]{1,0:T(8,128)S(1)}, f32[512,256]{1,0:T(8,128)S(1)}) fusion(f32[512,256]{1,0:T(8,128)S(1)} %get-tuple-element.249, f32[512]{0:T(512)S(1)} %neg.53, f32[512]{0:T(512)S(1)} %bitcast.90, f32[256]{0:T(256)S(1)} %bitcast.91, pred[]{:T(512)S(6)} %compare.5, pred[256]{0:T(512)(128)(4,1)S(1)} %compare_reduce_fusion.2, ...), kind=kLoop, calls=%fused_computation.8.clone.1 | loop fusion | flops 1179648 | bytes 2104577 | tf_op jit(solution)/shard_map/while/body/eval_jaxpr/add | solution.py:41
  7.2 2.4 %fusion.146 = (f32[512,256]{1,0:T(8,128)S(1)}, f32[512,256]{1,0:T(8,128)S(1)}) fusion(f32[512,256]{1,0:T(8,128)S(1)} %get-tuple-element.249, f32[512]{0:T(512)S(1)} %neg.53, f32[512]{0:T(512)S(1)} %bitcast.90, f32[256]{0:T(256)S(1)} %bitcast.91, pred[]{:T(512)S(6)} %compare.5, pred[256]{0:T(512)(128)(4,1)S(1)} %compare_reduce_fusion.2, ...), kind=kLoop, calls=%fused_computation.8.clone.1 | loop fusion | flops 1179648 | bytes 2104577 | tf_op jit(solution)/shard_map/while/body/eval_jaxpr/add | solution.py:41
  11.0 2.4 %fusion.146 = (f32[512,256]{1,0:T(8,128)S(1)}, f32[512,256]{1,0:T(8,128)S(1)}) fusion(f32[512,256]{1,0:T(8,128)S(1)} %get-tuple-element.249, f32[512]{0:T(512)S(1)} %neg.53, f32[512]{0:T(512)S(1)} %bitcast.90, f32[256]{0:T(256)S(1)} %bitcast.91, pred[]{:T(512)S(6)} %compare.5, pred[256]{0:T(512)(128)(4,1)S(1)} %compare_reduce_fusion.2, ...), kind=kLoop, calls=%fused_computation.8.clone.1 | loop fusion | flops 1179648 | bytes 2104577 | tf_op jit(solution)/shard_map/while/body/eval_jaxpr/add | solution.py:41
  14.8 2.4 %fusion.146 = (f32[512,256]{1,0:T(8,128)S(1)}, f32[512,256]{1,0:T(8,128)S(1)}) fusion(f32[512,256]{1,0:T(8,128)S(1)} %get-tuple-element.249, f32[512]{0:T(512)S(1)} %neg.53, f32[512]{0:T(512)S(1)} %bitcast.90, f32[256]{0:T(256)S(1)} %bitcast.91, pred[]{:T(512)S(6)} %compare.5, pred[256]{0:T(512)(128)(4,1)S(1)} %compare_reduce_fusion.2, ...), kind=kLoop, calls=%fused_computation.8.clone.1 | loop fusion | flops 1179648 | bytes 2104577 | tf_op jit(solution)/shard_map/while/body/eval_jaxpr/add | solution.py:41
  18.6 2.4 %fusion.146 = (f32[512,256]{1,0:T(8,128)S(1)}, f32[512,256]{1,0:T(8,128)S(1)}) fusion(f32[512,256]{1,0:T(8,128)S(1)} %get-tuple-element.249, f32[512]{0:T(512)S(1)} %neg.53, f32[512]{0:T(512)S(1)} %bitcast.90, f32[256]{0:T(256)S(1)} %bitcast.91, pred[]{:T(512)S(6)} %compare.5, pred[256]{0:T(512)(128)(4,1)S(1)} %compare_reduce_fusion.2, ...), kind=kLoop, calls=%fused_computation.8.clone.1 | loop fusion | flops 1179648 | bytes 2104577 | tf_op jit(solution)/shard_map/while/body/eval_jaxpr/add | solution.py:41
  22.4 2.4 %fusion.146 = (f32[512,256]{1,0:T(8,128)S(1)}, f32[512,256]{1,0:T(8,128)S(1)}) fusion(f32[512,256]{1,0:T(8,128)S(1)} %get-tuple-element.249, f32[512]{0:T(512)S(1)} %neg.53, f32[512]{0:T(512)S(1)} %bitcast.90, f32[256]{0:T(256)S(1)} %bitcast.91, pred[]{:T(512)S(6)} %compare.5, pred[256]{0:T(512)(128)(4,1)S(1)} %compare_reduce_fusion.2, ...), kind=kLoop, calls=%fused_computation.8.clone.1 | loop fusion | flops 1179648 | bytes 2104577 | tf_op jit(solution)/shard_map/while/body/eval_jaxpr/add | solution.py:41
  26.1 2.4 %fusion.146 = (f32[512,256]{1,0:T(8,128)S(1)}, f32[512,256]{1,0:T(8,128)S(1)}) fusion(f32[512,256]{1,0:T(8,128)S(1)} %get-tuple-element.249, f32[512]{0:T(512)S(1)} %neg.53, f32[512]{0:T(512)S(1)} %bitcast.90, f32[256]{0:T(256)S(1)} %bitcast.91, pred[]{:T(512)S(6)} %compare.5, pred[256]{0:T(512)(128)(4,1)S(1)} %compare_reduce_fusion.2, ...), kind=kLoop, calls=%fused_computation.8.clone.1 | loop fusion | flops 1179648 | bytes 2104577 | tf_op jit(solution)/shard_map/while/body/eval_jaxpr/add | solution.py:41
  29.9 2.4 %fusion.146 = (f32[512,256]{1,0:T(8,128)S(1)}, f32[512,256]{1,0:T(8,128)S(1)}) fusion(f32[512,256]{1,0:T(8,128)S(1)} %get-tuple-element.249, f32[512]{0:T(512)S(1)} %neg.53, f32[512]{0:T(512)S(1)} %bitcast.90, f32[256]{0:T(256)S(1)} %bitcast.91, pred[]{:T(512)S(6)} %compare.5, pred[256]{0:T(512)(128)(4,1)S(1)} %compare_reduce_fusion.2, ...), kind=kLoop, calls=%fused_computation.8.clone.1 | loop fusion | flops 1179648 | bytes 2104577 | tf_op jit(solution)/shard_map/while/body/eval_jaxpr/add | solution.py:41
  33.7 2.4 %fusion.146 = (f32[512,256]{1,0:T(8,128)S(1)}, f32[512,256]{1,0:T(8,128)S(1)}) fusion(f32[512,256]{1,0:T(8,128)S(1)} %get-tuple-element.249, f32[512]{0:T(512)S(1)} %neg.53, f32[512]{0:T(512)S(1)} %bitcast.90, f32[256]{0:T(256)S(1)} %bitcast.91, pred[]{:T(512)S(6)} %compare.5, pred[256]{0:T(512)(128)(4,1)S(1)} %compare_reduce_fusion.2, ...), kind=kLoop, calls=%fused_computation.8.clone.1 | loop fusion | flops 1179648 | bytes 2104577 | tf_op jit(solution)/shard_map/while/body/eval_jaxpr/add | solution.py:41
  37.5 2.4 %fusion.146 = (f32[512,256]{1,0:T(8,128)S(1)}, f32[512,256]{1,0:T(8,128)S(1)}) fusion(f32[512,256]{1,0:T(8,128)S(1)} %get-tuple-element.249, f32[512]{0:T(512)S(1)} %neg.53, f32[512]{0:T(512)S(1)} %bitcast.90, f32[256]{0:T(256)S(1)} %bitcast.91, pred[]{:T(512)S(6)} %compare.5, pred[256]{0:T(512)(128)(4,1)S(1)} %compare_reduce_fusion.2, ...), kind=kLoop, calls=%fused_computation.8.clone.1 | loop fusion | flops 1179648 | bytes 2104577 | tf_op jit(solution)/shard_map/while/body/eval_jaxpr/add | solution.py:41
  41.3 2.4 %fusion.146 = (f32[512,256]{1,0:T(8,128)S(1)}, f32[512,256]{1,0:T(8,128)S(1)}) fusion(f32[512,256]{1,0:T(8,128)S(1)} %get-tuple-element.249, f32[512]{0:T(512)S(1)} %neg.53, f32[512]{0:T(512)S(1)} %bitcast.90, f32[256]{0:T(256)S(1)} %bitcast.91, pred[]{:T(512)S(6)} %compare.5, pred[256]{0:T(512)(128)(4,1)S(1)} %compare_reduce_fusion.2, ...), kind=kLoop, calls=%fused_computation.8.clone.1 | loop fusion | flops 1179648 | bytes 2104577 | tf_op jit(solution)/shard_map/while/body/eval_jaxpr/add | solution.py:41
  45.1 2.4 %fusion.146 = (f32[512,256]{1,0:T(8,128)S(1)}, f32[512,256]{1,0:T(8,128)S(1)}) fusion(f32[512,256]{1,0:T(8,128)S(1)} %get-tuple-element.249, f32[512]{0:T(512)S(1)} %neg.53, f32[512]{0:T(512)S(1)} %bitcast.90, f32[256]{0:T(256)S(1)} %bitcast.91, pred[]{:T(512)S(6)} %compare.5, pred[256]{0:T(512)(128)(4,1)S(1)} %compare_reduce_fusion.2, ...), kind=kLoop, calls=%fused_computation.8.clone.1 | loop fusion | flops 1179648 | bytes 2104577 | tf_op jit(solution)/shard_map/while/body/eval_jaxpr/add | solution.py:41
  48.8 2.4 %fusion.146 = (f32[512,256]{1,0:T(8,128)S(1)}, f32[512,256]{1,0:T(8,128)S(1)}) fusion(f32[512,256]{1,0:T(8,128)S(1)} %get-tuple-element.249, f32[512]{0:T(512)S(1)} %neg.53, f32[512]{0:T(512)S(1)} %bitcast.90, f32[256]{0:T(256)S(1)} %bitcast.91, pred[]{:T(512)S(6)} %compare.5, pred[256]{0:T(512)(128)(4,1)S(1)} %compare_reduce_fusion.2, ...), kind=kLoop, calls=%fused_computation.8.clone.1 | loop fusion | flops 1179648 | bytes 2104577 | tf_op jit(solution)/shard_map/while/body/eval_jaxpr/add | solution.py:41
  52.6 2.4 %fusion.146 = (f32[512,256]{1,0:T(8,128)S(1)}, f32[512,256]{1,0:T(8,128)S(1)}) fusion(f32[512,256]{1,0:T(8,128)S(1)} %get-tuple-element.249, f32[512]{0:T(512)S(1)} %neg.53, f32[512]{0:T(512)S(1)} %bitcast.90, f32[256]{0:T(256)S(1)} %bitcast.91, pred[]{:T(512)S(6)} %compare.5, pred[256]{0:T(512)(128)(4,1)S(1)} %compare_reduce_fusion.2, ...), kind=kLoop, calls=%fused_computation.8.clone.1 | loop fusion | flops 1179648 | bytes 2104577 | tf_op jit(solution)/shard_map/while/body/eval_jaxpr/add | solution.py:41
  56.4 2.4 %fusion.146 = (f32[512,256]{1,0:T(8,128)S(1)}, f32[512,256]{1,0:T(8,128)S(1)}) fusion(f32[512,256]{1,0:T(8,128)S(1)} %get-tuple-element.249, f32[512]{0:T(512)S(1)} %neg.53, f32[512]{0:T(512)S(1)} %bitcast.90, f32[256]{0:T(256)S(1)} %bitcast.91, pred[]{:T(512)S(6)} %compare.5, pred[256]{0:T(512)(128)(4,1)S(1)} %compare_reduce_fusion.2, ...), kind=kLoop, calls=%fused_computation.8.clone.1 | loop fusion | flops 1179648 | bytes 2104577 | tf_op jit(solution)/shard_map/while/body/eval_jaxpr/add | solution.py:41
  60.2 2.4 %fusion.146 = (f32[512,256]{1,0:T(8,128)S(1)}, f32[512,256]{1,0:T(8,128)S(1)}) fusion(f32[512,256]{1,0:T(8,128)S(1)} %get-tuple-element.249, f32[512]{0:T(512)S(1)} %neg.53, f32[512]{0:T(512)S(1)} %bitcast.90, f32[256]{0:T(256)S(1)} %bitcast.91, pred[]{:T(512)S(6)} %compare.5, pred[256]{0:T(512)(128)(4,1)S(1)} %compare_reduce_fusion.2, ...), kind=kLoop, calls=%fused_computation.8.clone.1 | loop fusion | flops 1179648 | bytes 2104577 | tf_op jit(solution)/shard_map/while/body/eval_jaxpr/add | solution.py:41
  64.0 2.4 %fusion.146 = (f32[512,256]{1,0:T(8,128)S(1)}, f32[512,256]{1,0:T(8,128)S(1)}) fusion(f32[512,256]{1,0:T(8,128)S(1)} %get-tuple-element.249, f32[512]{0:T(512)S(1)} %neg.53, f32[512]{0:T(512)S(1)} %bitcast.90, f32[256]{0:T(256)S(1)} %bitcast.91, pred[]{:T(512)S(6)} %compare.5, pred[256]{0:T(512)(128)(4,1)S(1)} %compare_reduce_fusion.2, ...), kind=kLoop, calls=%fused_computation.8.clone.1 | loop fusion | flops 1179648 | bytes 2104577 | tf_op jit(solution)/shard_map/while/body/eval_jaxpr/add | solution.py:41
  67.8 2.4 %fusion.146 = (f32[512,256]{1,0:T(8,128)S(1)}, f32[512,256]{1,0:T(8,128)S(1)}) fusion(f32[512,256]{1,0:T(8,128)S(1)} %get-tuple-element.249, f32[512]{0:T(512)S(1)} %neg.53, f32[512]{0:T(512)S(1)} %bitcast.90, f32[256]{0:T(256)S(1)} %bitcast.91, pred[]{:T(512)S(6)} %compare.5, pred[256]{0:T(512)(128)(4,1)S(1)} %compare_reduce_fusion.2, ...), kind=kLoop, calls=%fused_computation.8.clone.1 | loop fusion | flops 1179648 | bytes 2104577 | tf_op jit(solution)/shard_map/while/body/eval_jaxpr/add | solution.py:41
  71.5 2.4 %fusion.146 = (f32[512,256]{1,0:T(8,128)S(1)}, f32[512,256]{1,0:T(8,128)S(1)}) fusion(f32[512,256]{1,0:T(8,128)S(1)} %get-tuple-element.249, f32[512]{0:T(512)S(1)} %neg.53, f32[512]{0:T(512)S(1)} %bitcast.90, f32[256]{0:T(256)S(1)} %bitcast.91, pred[]{:T(512)S(6)} %compare.5, pred[256]{0:T(512)(128)(4,1)S(1)} %compare_reduce_fusion.2, ...), kind=kLoop, calls=%fused_computation.8.clone.1 | loop fusion | flops 1179648 | bytes 2104577 | tf_op jit(solution)/shard_map/while/body/eval_jaxpr/add | solution.py:41
  75.3 2.4 %fusion.146 = (f32[512,256]{1,0:T(8,128)S(1)}, f32[512,256]{1,0:T(8,128)S(1)}) fusion(f32[512,256]{1,0:T(8,128)S(1)} %get-tuple-element.249, f32[512]{0:T(512)S(1)} %neg.53, f32[512]{0:T(512)S(1)} %bitcast.90, f32[256]{0:T(256)S(1)} %bitcast.91, pred[]{:T(512)S(6)} %compare.5, pred[256]{0:T(512)(128)(4,1)S(1)} %compare_reduce_fusion.2, ...), kind=kLoop, calls=%fused_computation.8.clone.1 | loop fusion | flops 1179648 | bytes 2104577 | tf_op jit(solution)/shard_map/while/body/eval_jaxpr/add | solution.py:41
  79.1 2.4 %fusion.146 = (f32[512,256]{1,0:T(8,128)S(1)}, f32[512,256]{1,0:T(8,128)S(1)}) fusion(f32[512,256]{1,0:T(8,128)S(1)} %get-tuple-element.249, f32[512]{0:T(512)S(1)} %neg.53, f32[512]{0:T(512)S(1)} %bitcast.90, f32[256]{0:T(256)S(1)} %bitcast.91, pred[]{:T(512)S(6)} %compare.5, pred[256]{0:T(512)(128)(4,1)S(1)} %compare_reduce_fusion.2, ...), kind=kLoop, calls=%fused_computation.8.clone.1 | loop fusion | flops 1179648 | bytes 2104577 | tf_op jit(solution)/shard_map/while/body/eval_jaxpr/add | solution.py:41
  82.9 2.4 %fusion.146 = (f32[512,256]{1,0:T(8,128)S(1)}, f32[512,256]{1,0:T(8,128)S(1)}) fusion(f32[512,256]{1,0:T(8,128)S(1)} %get-tuple-element.249, f32[512]{0:T(512)S(1)} %neg.53, f32[512]{0:T(512)S(1)} %bitcast.90, f32[256]{0:T(256)S(1)} %bitcast.91, pred[]{:T(512)S(6)} %compare.5, pred[256]{0:T(512)(128)(4,1)S(1)} %compare_reduce_fusion.2, ...), kind=kLoop, calls=%fused_computation.8.clone.1 | loop fusion | flops 1179648 | bytes 2104577 | tf_op jit(solution)/shard_map/while/body/eval_jaxpr/add | solution.py:41
  86.7 2.4 %fusion.146 = (f32[512,256]{1,0:T(8,128)S(1)}, f32[512,256]{1,0:T(8,128)S(1)}) fusion(f32[512,256]{1,0:T(8,128)S(1)} %get-tuple-element.249, f32[512]{0:T(512)S(1)} %neg.53, f32[512]{0:T(512)S(1)} %bitcast.90, f32[256]{0:T(256)S(1)} %bitcast.91, pred[]{:T(512)S(6)} %compare.5, pred[256]{0:T(512)(128)(4,1)S(1)} %compare_reduce_fusion.2, ...), kind=kLoop, calls=%fused_computation.8.clone.1 | loop fusion | flops 1179648 | bytes 2104577 | tf_op jit(solution)/shard_map/while/body/eval_jaxpr/add | solution.py:41
  90.4 2.4 %fusion.146 = (f32[512,256]{1,0:T(8,128)S(1)}, f32[512,256]{1,0:T(8,128)S(1)}) fusion(f32[512,256]{1,0:T(8,128)S(1)} %get-tuple-element.249, f32[512]{0:T(512)S(1)} %neg.53, f32[512]{0:T(512)S(1)} %bitcast.90, f32[256]{0:T(256)S(1)} %bitcast.91, pred[]{:T(512)S(6)} %compare.5, pred[256]{0:T(512)(128)(4,1)S(1)} %compare_reduce_fusion.2, ...), kind=kLoop, calls=%fused_computation.8.clone.1 | loop fusion | flops 1179648 | bytes 2104577 | tf_op jit(solution)/shard_map/while/body/eval_jaxpr/add | solution.py:41
  94.2 2.4 %fusion.146 = (f32[512,256]{1,0:T(8,128)S(1)}, f32[512,256]{1,0:T(8,128)S(1)}) fusion(f32[512,256]{1,0:T(8,128)S(1)} %get-tuple-element.249, f32[512]{0:T(512)S(1)} %neg.53, f32[512]{0:T(512)S(1)} %bitcast.90, f32[256]{0:T(256)S(1)} %bitcast.91, pred[]{:T(512)S(6)} %compare.5, pred[256]{0:T(512)(128)(4,1)S(1)} %compare_reduce_fusion.2, ...), kind=kLoop, calls=%fused_computation.8.clone.1 | loop fusion | flops 1179648 | bytes 2104577 | tf_op jit(solution)/shard_map/while/body/eval_jaxpr/add | solution.py:41
  98.0 2.4 %fusion.146 = (f32[512,256]{1,0:T(8,128)S(1)}, f32[512,256]{1,0:T(8,128)S(1)}) fusion(f32[512,256]{1,0:T(8,128)S(1)} %get-tuple-element.249, f32[512]{0:T(512)S(1)} %neg.53, f32[512]{0:T(512)S(1)} %bitcast.90, f32[256]{0:T(256)S(1)} %bitcast.91, pred[]{:T(512)S(6)} %compare.5, pred[256]{0:T(512)(128)(4,1)S(1)} %compare_reduce_fusion.2, ...), kind=kLoop, calls=%fused_computation.8.clone.1 | loop fusion | flops 1179648 | bytes 2104577 | tf_op jit(solution)/shard_map/while/body/eval_jaxpr/add | solution.py:41
  101.8 2.4 %fusion.146 = (f32[512,256]{1,0:T(8,128)S(1)}, f32[512,256]{1,0:T(8,128)S(1)}) fusion(f32[512,256]{1,0:T(8,128)S(1)} %get-tuple-element.249, f32[512]{0:T(512)S(1)} %neg.53, f32[512]{0:T(512)S(1)} %bitcast.90, f32[256]{0:T(256)S(1)} %bitcast.91, pred[]{:T(512)S(6)} %compare.5, pred[256]{0:T(512)(128)(4,1)S(1)} %compare_reduce_fusion.2, ...), kind=kLoop, calls=%fused_computation.8.clone.1 | loop fusion | flops 1179648 | bytes 2104577 | tf_op jit(solution)/shard_map/while/body/eval_jaxpr/add | solution.py:41
  105.6 2.4 %fusion.146 = (f32[512,256]{1,0:T(8,128)S(1)}, f32[512,256]{1,0:T(8,128)S(1)}) fusion(f32[512,256]{1,0:T(8,128)S(1)} %get-tuple-element.249, f32[512]{0:T(512)S(1)} %neg.53, f32[512]{0:T(512)S(1)} %bitcast.90, f32[256]{0:T(256)S(1)} %bitcast.91, pred[]{:T(512)S(6)} %compare.5, pred[256]{0:T(512)(128)(4,1)S(1)} %compare_reduce_fusion.2, ...), kind=kLoop, calls=%fused_computation.8.clone.1 | loop fusion | flops 1179648 | bytes 2104577 | tf_op jit(solution)/shard_map/while/body/eval_jaxpr/add | solution.py:41
  109.4 2.4 %fusion.146 = (f32[512,256]{1,0:T(8,128)S(1)}, f32[512,256]{1,0:T(8,128)S(1)}) fusion(f32[512,256]{1,0:T(8,128)S(1)} %get-tuple-element.249, f32[512]{0:T(512)S(1)} %neg.53, f32[512]{0:T(512)S(1)} %bitcast.90, f32[256]{0:T(256)S(1)} %bitcast.91, pred[]{:T(512)S(6)} %compare.5, pred[256]{0:T(512)(128)(4,1)S(1)} %compare_reduce_fusion.2, ...), kind=kLoop, calls=%fused_computation.8.clone.1 | loop fusion | flops 1179648 | bytes 2104577 | tf_op jit(solution)/shard_map/while/body/eval_jaxpr/add | solution.py:41
  113.1 2.4 %fusion.146 = (f32[512,256]{1,0:T(8,128)S(1)}, f32[512,256]{1,0:T(8,128)S(1)}) fusion(f32[512,256]{1,0:T(8,128)S(1)} %get-tuple-element.249, f32[512]{0:T(512)S(1)} %neg.53, f32[512]{0:T(512)S(1)} %bitcast.90, f32[256]{0:T(256)S(1)} %bitcast.91, pred[]{:T(512)S(6)} %compare.5, pred[256]{0:T(512)(128)(4,1)S(1)} %compare_reduce_fusion.2, ...), kind=kLoop, calls=%fused_computation.8.clone.1 | loop fusion | flops 1179648 | bytes 2104577 | tf_op jit(solution)/shard_map/while/body/eval_jaxpr/add | solution.py:41
  116.9 2.4 %fusion.146 = (f32[512,256]{1,0:T(8,128)S(1)}, f32[512,256]{1,0:T(8,128)S(1)}) fusion(f32[512,256]{1,0:T(8,128)S(1)} %get-tuple-element.249, f32[512]{0:T(512)S(1)} %neg.53, f32[512]{0:T(512)S(1)} %bitcast.90, f32[256]{0:T(256)S(1)} %bitcast.91, pred[]{:T(512)S(6)} %compare.5, pred[256]{0:T(512)(128)(4,1)S(1)} %compare_reduce_fusion.2, ...), kind=kLoop, calls=%fused_computation.8.clone.1 | loop fusion | flops 1179648 | bytes 2104577 | tf_op jit(solution)/shard_map/while/body/eval_jaxpr/add | solution.py:41
  120.7 2.4 %fusion.146 = (f32[512,256]{1,0:T(8,128)S(1)}, f32[512,256]{1,0:T(8,128)S(1)}) fusion(f32[512,256]{1,0:T(8,128)S(1)} %get-tuple-element.249, f32[512]{0:T(512)S(1)} %neg.53, f32[512]{0:T(512)S(1)} %bitcast.90, f32[256]{0:T(256)S(1)} %bitcast.91, pred[]{:T(512)S(6)} %compare.5, pred[256]{0:T(512)(128)(4,1)S(1)} %compare_reduce_fusion.2, ...), kind=kLoop, calls=%fused_computation.8.clone.1 | loop fusion | flops 1179648 | bytes 2104577 | tf_op jit(solution)/shard_map/while/body/eval_jaxpr/add | solution.py:41
  123.1 2.9 %fusion.38 = (f32[512,256]{1,0:T(8,128)S(1)}, f32[512,256]{1,0:T(8,128)S(1)}) fusion(f32[512,256]{1,0:T(8,128)S(1)} %get-tuple-element.116, f32[256]{0:T(256)S(1)} %fusion.101, f32[256]{0:T(256)S(1)} %get-tuple-element.180, f32[256]{0:T(256)S(1)} %get-tuple-element.183, f32[256]{0:T(256)S(1)} %get-tuple-element.179, f32[256]{0:T(256)S(1)} %get-tuple-element.184, ...), kind=kLoop, calls=%fused_computation.82 | loop fusion | flops 5636096 | bytes 2105344 | tf_op jit(solution)/shard_map/sub | solution.py:59
  126.0 5.6 %fusion.65 = f32[512,256]{1,0:T(8,128)S(1)} fusion(f32[512,256]{1,0:T(8,128)S(1)} %get-tuple-element.176), kind=kOutput, calls=%fused_computation.113 | convolution fusion | flops 808976384 | bytes 1048576 | tf_op jit(solution)/shard_map/dot_general | solution.py:78
  131.6 5.6 %fusion.63 = f32[512,256]{1,0:T(8,128)S(1)} fusion(f32[512,256]{1,0:T(8,128)S(1)} %get-tuple-element.176), kind=kOutput, calls=%fused_computation.112 | convolution fusion | flops 808976384 | bytes 1048576 | tf_op jit(solution)/shard_map/dot_general | solution.py:78
  137.3 5.6 %convolution_add_fusion = f32[512,256]{1,0:T(8,128)S(1)} fusion(f32[512,256]{1,0:T(8,128)S(1)} %fusion.65, f32[512,256]{1,0:T(8,128)S(1)} %get-tuple-element.175), kind=kOutput, calls=%fused_computation.32 | convolution fusion | flops 809107456 | bytes 1572864 | tf_op jit(solution)/shard_map/dot_general | solution.py:78
  142.9 7.2 %subtract_bitcast_fusion.1 = (f32[1,512,256]{2,1,0:T(8,128)S(1)}, f32[1,512,256]{2,1,0:T(8,128)S(1)}) fusion(f32[512,256]{1,0:T(8,128)S(1)} %convolution_add_fusion, f32[512]{0:T(512)S(1)} %get-tuple-element.185, f32[512]{0:T(512)S(1)} %get-tuple-element.186, f32[512,256]{1,0:T(8,128)S(1)} %fusion.63, f32[512,256]{1,0:T(8,128)S(1)} %get-tuple-element.175), kind=kOutput, calls=%fused_computation.109 | convolution fusion | flops 809893888 | bytes 2625536 | tf_op jit(solution)/shard_map/dot_general | solution.py:78
  155.5 7.3 %all-to-all-start = ((f32[8,2,1,64,256]{4,3,1,2,0:T(8,128)}), f32[8,2,1,64,256]{4,3,1,2,0:T(8,128)S(1)}, u32[]{:S(2)}, u32[]{:S(2)}) async-start(f32[8,2,1,64,256]{4,3,1,2,0:T(8,128)} %fusion.74), calls=%async_computation | async-start | bytes 2097152 | tf_op jit(solution)/shard_map/all_to_all | solution.py:116
  162.8 25.7 %all-to-all-done = f32[8,2,1,64,256]{4,3,1,2,0:T(8,128)S(1)} async-done(((f32[8,2,1,64,256]{4,3,1,2,0:T(8,128)}), f32[8,2,1,64,256]{4,3,1,2,0:T(8,128)S(1)}, u32[]{:S(2)}, u32[]{:S(2)}) %all-to-all-start) | async-done | bytes 1048608 | tf_op jit(solution)/shard_map/all_to_all | solution.py:116
  188.6 0.8 fusion.70
  191.1 1.0 add_bitcast_fusion
  192.3 1.3 collective-permute-start
  193.6 1.3 collective-permute-start.1
  195.1 2.3 %collective-permute-done.1 = f32[2,8,64,8]{3,1,2,0:T(8,128)S(1)} collective-permute-done((f32[2,8,64,8]{3,1,2,0:T(8,128)S(1)}, f32[2,8,64,8]{3,1,2,0:T(8,128)S(1)}, u32[]{:S(2)}, u32[]{:S(2)}) %collective-permute-start.1) | collective-permute-done | bytes 32800 | tf_op jit(solution)/shard_map/ppermute | solution.py:20
  197.9 4.2 %fusion.30 = (f32[2,8,64,256,1]{3,1,2,0,4:T(8,128)S(1)}, f32[2,8,64,256,1]{3,1,2,0,4:T(8,128)S(1)}) fusion(f32[1,8,64,256]{3,1,2,0:T(8,128)S(1)} %get-tuple-element.165, f32[1,8,64,256]{3,1,2,0:T(8,128)S(1)} %get-tuple-element.166, f32[2,8,64,264]{3,1,2,0:T(8,128)S(1)} %get-tuple-element.170, f32[2,8,64,264]{3,1,2,0:T(8,128)S(1)} %get-tuple-element.169), kind=kLoop, calls=%fused_computation.74 | loop fusion | flops 8388608 | bytes 18874368 | tf_op jit(solution)/shard_map/stack | solution.py:73
  202.3 3.9 %copy.12 = f32[2,8,64,256,2]{2,1,4,3,0:T(8,128)} copy(f32[2,8,64,256,2]{3,1,2,0,4:T(8,128)S(1)} %pad_maximum_fusion) | data formatting | bytes 4194304 | tf_op jit(solution)/shard_map/stack | solution.py:73
  206.2 3.8 %copy.13 = f32[2,8,64,512]{3,2,1,0:T(8,128)} copy(f32[2,8,64,512]{2,1,3,0:T(8,128)} %bitcast.86) | data formatting | bytes 4194304 | tf_op jit(solution)/shard_map/reshape | solution.py:74
  (153 shorter events, 53.6 us)
Async XLA Ops:
  155.5 33.0 %all-to-all-start = ((f32[8,2,1,64,256]{4,3,1,2,0:T(8,128)}), f32[8,2,1,64,256]{4,3,1,2,0:T(8,128)S(1)}, u32[]{:S(2)}, u32[]{:S(2)}) async-start(f32[8,2,1,64,256]{4,3,1,2,0:T(8,128)} %fusion.74), calls=%async_computation | async-start | bytes 2097152 | tf_op jit(solution)/shard_map/all_to_all | solution.py:116
  192.3 2.8 %collective-permute-start = (f32[2,8,64,8]{3,1,2,0:T(8,128)S(1)}, f32[2,8,64,8]{3,1,2,0:T(8,128)S(1)}, u32[]{:S(2)}, u32[]{:S(2)}) collective-permute-start(f32[2,8,64,8]{3,1,2,0:T(8,128)S(1)} %get-tuple-element.171), channel_id=1, source_target_pairs={{0,1},{2,3},{4,5},{6,7},{8,9},{10,11},{12,13},{14,15},{16,17},{18,... | collective-permute-start | bytes 98312 | tf_op jit(solution)/shard_map/ppermute | solution.py:17
  193.6 3.8 %collective-permute-start.1 = (f32[2,8,64,8]{3,1,2,0:T(8,128)S(1)}, f32[2,8,64,8]{3,1,2,0:T(8,128)S(1)}, u32[]{:S(2)}, u32[]{:S(2)}) collective-permute-start(f32[2,8,64,8]{3,1,2,0:T(8,128)S(1)} %get-tuple-element.172), channel_id=1, source_target_pairs={{1,0},{3,2},{5,4},{7,6},{9,8},{11,10},{13,12},{15,14},{17,16},{19,... | collective-permute-start | bytes 98312 | tf_op jit(solution)/shard_map/ppermute | solution.py:20
